TPU v7x, 32 devices: a whole 2x2x4 slice. The times are simulated.
32 devices in a mesh: dp: 8 (over z, x), tm: 4 (over y, core).
Axes of the slice: x: 2, y: 2, z: 4, core: 2. Of those that a mesh axis runs over, the one named last changes fastest.
Arguments:
- clip_input: bfloat16 [8, 8, 256, 384], P('dp', 'tm'), may hold values from -32 to 32
- norm_gain: float32 [384], replicated, may hold values from 0.1 to 1.9
- qkv_weight: bfloat16 [384, 1152], replicated, may hold values from -2 to 2
- out_weight: bfloat16 [384, 384], replicated, may hold values from -0.3125 to 0.3125
- time_weight: bfloat16 [3, 384, 768], P(None, 'dp'), may hold values from -0.1875 to 0.1875
- upsample_cotangent: bfloat16 [8, 8, 256, 768], P('dp', 'tm'), may hold values from -6 to 6
Outputs:
- input_grad: bfloat16 [8, 8, 256, 384], P('dp', 'tm')
- qkv_grad: float32 [384, 1152], P('dp', 'tm')
All inputs are finite; a program needn't handle non-finite values.
Results may differ from a plain program's by a relative error of at most 0.024.
Values may be sent and summed in bfloat16 or wider, within the bound.
A program may use at most 64 MiB of HBM per device.

v0:
```python
import math

import jax
import jax.numpy as jnp
from jax import lax
from jax.sharding import PartitionSpec as P


def passed_along(block, axis, distance):
    devices = range(lax.axis_size(axis))
    route = [(i - distance, i) for i in devices if i - distance in devices]
    return lax.ppermute(block, axis, route)


def rms_scaled(features, norm_gain):
    squares = jnp.mean(features * features, axis=-1, keepdims=True)
    return features * lax.rsqrt(squares + 1e-06) * norm_gain


def block_tail(qkv_rows, features, out_weight):
    width = features.shape[-1]
    queries = qkv_rows[..., :width]
    keys = qkv_rows[..., width : 2 * width]
    values = qkv_rows[..., 2 * width :]
    scores = jnp.einsum(
        "fqc,fkc->fqk", queries, keys, preferred_element_type=jnp.float32
    ) / math.sqrt(width)
    weights = jax.nn.softmax(scores, axis=-1).astype(jnp.bfloat16)
    mixed = jnp.einsum("fqk,fkc->fqc", weights, values, preferred_element_type=jnp.float32).astype(
        jnp.bfloat16
    )
    branch = jnp.einsum("fqc,cd->fqd", mixed, out_weight, preferred_element_type=jnp.float32)
    return (features + branch).astype(jnp.bfloat16)


def attention_grads(clip_rows, norm_gain, qkv_weight, out_weight, upstream):
    features = clip_rows.astype(jnp.float32)
    normed, pre_back = jax.vjp(lambda value: rms_scaled(value, norm_gain), features)
    normed_bf = normed.astype(jnp.bfloat16)
    qkv_rows = jnp.einsum(
        "fhc,cd->fhd", normed_bf, qkv_weight, preferred_element_type=jnp.float32
    ).astype(jnp.bfloat16)
    block_out, tail_back = jax.vjp(
        lambda first, second: block_tail(first, second, out_weight), qkv_rows, features
    )
    qkv_cot, feature_cot = tail_back(upstream)
    normed_cot = jnp.einsum("fhd,cd->fhc", qkv_cot, qkv_weight, preferred_element_type=jnp.float32)
    direct = pre_back(normed_cot)[0]
    input_grad = (feature_cot + direct).astype(jnp.bfloat16)
    return (input_grad, normed_bf, qkv_cot)


def on_device(clip_input, norm_gain, qkv_weight, out_weight, time_weight, upsample_cotangent):
    rows = clip_input[0]
    cotangent = upsample_cotangent[0]
    frames = cotangent.shape[0]
    width = rows.shape[-1]
    incoming = passed_along(cotangent, "tm", -1)
    padded = jnp.concatenate([cotangent, incoming], 0)
    piece = lax.all_gather(time_weight, "dp", axis=1, tiled=True)
    result = jnp.einsum(
        "fhd,cd->fhc", padded[2 : 2 + frames], piece[0], preferred_element_type=jnp.float32
    )
    result = result + jnp.einsum(
        "fhd,cd->fhc", padded[1 : 1 + frames], piece[1], preferred_element_type=jnp.float32
    )
    upstream = (
        result
        + jnp.einsum("fhd,cd->fhc", padded[0:frames], piece[2], preferred_element_type=jnp.float32)
    ).astype(jnp.bfloat16)
    input_grad, normed_bf, qkv_cot = attention_grads(
        rows, norm_gain, qkv_weight, out_weight, upstream
    )
    flat_normed = normed_bf.reshape(-1, width)
    flat_cot = qkv_cot.reshape(-1, 3 * width)
    shares = lax.psum_scatter(
        jnp.einsum("rc,rd->cd", flat_normed, flat_cot, preferred_element_type=jnp.float32).astype(
            jnp.bfloat16
        ),
        "dp",
        scatter_dimension=0,
        tiled=True,
    )
    qkv_grad = lax.psum_scatter(shares, "tm", scatter_dimension=1, tiled=True).astype(jnp.float32)
    return (input_grad[None], qkv_grad)


def solution(mesh):
    in_specs = (
        P("dp", "tm", None, None),
        P(),
        P(),
        P(),
        P(None, "dp", None),
        P("dp", "tm", None, None),
    )
    out_specs = (P("dp", "tm", None, None), P("dp", "tm"))
    return jax.shard_map(
        on_device, mesh=mesh, in_specs=in_specs, out_specs=out_specs, check_vma=False
    )
```

profile of v0, /device:TPU:0, one launch (start us, length us, event | category | flops | bytes accessed | tf_op | source)
XLA Modules:
  0.0 162.2 jit_solution(4110133302640648033)
XLA Ops:
  7.2 0.0 copy-start
  7.2 0.0 all-gather.2.cloned.1.call-start
  7.2 0.7 all-gather.2.cloned.1.call-update
  7.9 0.0 reduce-scatter.5.cloned.1.call-start
  8.0 1.3 collective-permute-start
  9.3 1.1 fusion.15
  10.4 0.0 copy-done
  10.4 1.9 %convolution_convert_fusion = bf16[2,256,1152]{2,1,0:T(8,128)(2,1)S(1)} fusion(bf16[384,1152]{1,0:T(8,128)(2,1)S(1)} %copy-done, bf16[1,2,256,384]{3,2,1,0:T(8,128)(2,1)} %param.6, f32[384]{0:T(512)} %param.7, f32[2,256]{1,0:T(2,128)S(1)} %fusion.30), kind=kOutput, calls=%fused_computation.1 | convolution fusion | flops 454361088 | bytes 2461184 | tf_op jit(solution)/shard_map/fhc,cd->fhd/dot_general | solution.py:40
  12.3 0.0 copy-start.2
  12.3 1.0 copy-done.2
  13.3 0.0 copy-start.3
  13.4 0.3 convolution_multiply_fusion.1
  13.7 0.4 fusion.36
  14.1 44.8 %all-gather.2.cloned.1.call-done = bf16[3,384,768]{2,1,0:T(8,128)(2,1)} async-done(((bf16[3,48,768]{2,1,0:T(8,128)(2,1)}), bf16[3,384,768]{2,1,0:T(8,128)(2,1)}) %all-gather.2.cloned.1.call-update) | async-done | bytes 1769488 | tf_op jit(solution)/shard_map/all_gather | solution.py:60
  58.9 0.0 copy-done.3
  58.9 0.0 copy-start.4
  58.9 1.8 %fusion.19 = f32[2,256,384]{2,1,0:T(8,128)S(1)} fusion(bf16[3,384,768]{2,1,0:T(8,128)(2,1)} %all-gather.2.cloned.1.call-done, bf16[1,2,256,768]{3,2,1,0:T(8,128)(2,1)S(1)} %copy-done.3), kind=kOutput, calls=%fused_computation.36 | convolution fusion | flops 301989888 | bytes 2162688 | tf_op jit(solution)/shard_map/fhd,cd->fhc/dot_general | solution.py:69
  60.7 0.0 collective-permute-done
  60.7 0.0 copy-done.4
  60.7 0.6 fusion.2
  61.3 0.0 copy-start.6
  61.3 0.6 fusion.8
  61.9 0.3 copy-done.6
  62.2 0.4 convolution_convert_fusion.4
  62.7 2.1 %multiply_reduce_fusion = (f32[2,256]{1,0:T(2,128)S(1)}, f32[2,256,256]{1,2,0:T(8,128)}) fusion(f32[2,256,256]{1,2,0:T(8,128)S(1)} %get-tuple-element.3, f32[2,256]{1,0:T(2,128)S(1)} %multiply_divide_fusion, bf16[2,256,384]{2,1,0:T(8,128)(2,1)S(1)} %convolution_convert_fusion.4, bf16[2,256,1152]{2,1,0:T(8,128)(2,1)} %copy-done.2), kind=kOutput, calls=%fused_computation.40 | convolution fusion | flops 101318144 | bytes 1839104 | tf_op jit(solution)/shard_map/transpose(jvp(fqk,fkc->fqc))/dot_general | solution.py:29
  64.8 0.0 copy-start.5
  64.8 2.3 %convolution_convert_fusion.2 = bf16[2,256,384]{2,1,0:T(8,128)(2,1)} fusion(bf16[2,256,1152]{2,1,0:T(8,128)(2,1)} %copy-done.2, f32[2,256,256]{1,2,0:T(8,128)} %get-tuple-element.5, f32[2,256]{1,0:T(2,128)S(1)} %neg.6, f32[2,256]{1,0:T(2,128)S(1)} %get-tuple-element.2, f32[2,256,256]{1,2,0:T(8,128)S(1)} %convolution_multiply_fusion.1), kind=kOutput, calls=%fused_computation.18 | convolution fusion | flops 101516032 | bytes 2363392 | tf_op jit(solution)/shard_map/transpose(jvp(fqc,fkc->fqk))/dot_general | solution.py:25
  67.1 0.0 copy-done.5
  67.1 1.4 convolution_convert_fusion.1
  68.6 0.0 copy-start.1
  68.6 0.0 copy-start.7
  68.6 0.3 convolution_convert_fusion.3
  69.0 0.6 copy-done.1
  69.6 0.0 copy-done.7
  69.6 2.7 %fusion.1 = bf16[384,1152]{1,0:T(8,128)(2,1)} fusion(bf16[2,256,384]{2,1,0:T(8,128)(2,1)S(1)} %convolution_convert_fusion.1, bf16[2,256,384]{2,1,0:T(8,128)(2,1)} %convolution_convert_fusion.2, bf16[2,256,384]{2,1,0:T(8,128)(2,1)S(1)} %convolution_convert_fusion.3, bf16[1,2,256,384]{3,2,1,0:T(8,128)(2,1)S(1)} %copy-done.1, f32[384]{0:T(512)S(1)} %copy-done.7, ...), kind=kOutput, calls=%fused_computation.3 | convolution fusion | flops 457752576 | bytes 2461184 | tf_op jit(solution)/shard_map/rc,rd->cd/dot_general | solution.py:77
  72.3 0.0 reduce-scatter.5.cloned.1.call-update
  72.3 0.0 reduce-scatter.7.cloned.1.call-start
  72.4 1.9 %fusion.18 = (f32[2,256]{1,0:T(2,128)S(1)}, f32[2,256,384]{2,1,0:T(8,128)S(1)}) fusion(bf16[1,2,256,384]{3,2,1,0:T(8,128)(2,1)S(1)} %copy-done.1, f32[384]{0:T(512)S(1)} %copy-done.7, bf16[384,1152]{1,0:T(8,128)(2,1)S(1)} %copy-done, bf16[2,256,384]{2,1,0:T(8,128)(2,1)S(1)} %convolution_convert_fusion.1, ...), kind=kOutput, calls=%fused_computation.34 | convolution fusion | flops 457309696 | bytes 3247616 | tf_op jit(solution)/shard_map/fhd,cd->fhc/dot_general | solution.py:47
  74.3 58.0 %reduce-scatter.5.cloned.1.call-done = bf16[48,1152]{1,0:T(8,128)(2,1)} async-done(((bf16[384,1152]{1,0:T(8,128)(2,1)}), bf16[48,1152]{1,0:T(8,128)(2,1)}) %reduce-scatter.5.cloned.1.call-update) | async-done | bytes 110608 | tf_op jit(solution)/shard_map/reduce_scatter | solution.py:76
  132.3 1.8 %copy.14 = bf16[48,1152]{0,1:T(8,128)(2,1)} copy(bf16[48,1152]{1,0:T(8,128)(2,1)} %reduce-scatter.5.cloned.1.call-done) | data formatting | bytes 221184
  134.1 0.0 reduce-scatter.7.cloned.1.call-update
  134.1 1.0 fusion.20
  135.1 18.9 %reduce-scatter.7.cloned.1.call-done = bf16[288,48]{1,0:T(8,128)(2,1)} async-done(((bf16[1152,48]{1,0:T(8,128)(2,1)}), bf16[288,48]{1,0:T(8,128)(2,1)}) %reduce-scatter.7.cloned.1.call-update) | async-done | bytes 27664
  154.0 1.0 copy.15
  155.0 0.6 convert_element_type.64
  (4 shorter events, 0.0 us)
Async XLA Ops:
  7.2 3.3 %copy-start = (bf16[384,1152]{1,0:T(8,128)(2,1)S(1)}, bf16[384,1152]{1,0:T(8,128)(2,1)}, u32[]{:S(2)}) copy-start(bf16[384,1152]{1,0:T(8,128)(2,1)} %param.8) | copy-start | bytes 2654212
  7.2 51.7 %all-gather.2.cloned.1.call-start = ((), (), s32[]{:S(2)}) async-start(), calls=%async_computation.2 | async-start | bytes 1990656 | tf_op jit(solution)/shard_map/all_gather | solution.py:60
  7.9 124.4 %reduce-scatter.5.cloned.1.call-start = ((), (), s32[]{:S(2)}) async-start(), calls=%async_computation.3 | async-start | bytes 995328 | tf_op jit(solution)/shard_map/reduce_scatter | solution.py:76
  8.0 52.7 %collective-permute-start = (bf16[2,256,768]{2,1,0:T(8,128)(2,1)}, bf16[2,256,768]{2,1,0:T(8,128)(2,1)S(1)}, u32[]{:S(2)}, u32[]{:S(2)}) collective-permute-start(bf16[2,256,768]{2,1,0:T(8,128)(2,1)} %bitcast.50), channel_id=1, source_target_pairs={{1,0},{2,1},{3,2},{5,4},{6,5},{7,6},{9,8},{10,9},{11,10},{13,12},{... | collective-permute-start | bytes 2359304 | tf_op jit(solution)/shard_map/ppermute | solution.py:12
  12.3 1.0 copy-start.2
  13.3 45.5 %copy-start.3 = (bf16[1,2,256,768]{3,2,1,0:T(8,128)(2,1)S(1)}, bf16[1,2,256,768]{3,2,1,0:T(8,128)(2,1)}, u32[]{:S(2)}) copy-start(bf16[1,2,256,768]{3,2,1,0:T(8,128)(2,1)} %param.11) | copy-start | bytes 2359300
  58.9 1.8 %copy-start.4 = (bf16[3,384,768]{2,1,0:T(8,128)(2,1)S(1)}, bf16[3,384,768]{2,1,0:T(8,128)(2,1)}, u32[]{:S(2)}) copy-start(bf16[3,384,768]{2,1,0:T(8,128)(2,1)} %all-gather.2.cloned.1.call-done) | copy-start | bytes 5308420
  61.3 1.0 copy-start.6
  64.8 2.4 %copy-start.5 = (f32[2,256,256]{1,2,0:T(8,128)S(1)}, f32[2,256,256]{1,2,0:T(8,128)}, u32[]{:S(2)}) copy-start(f32[2,256,256]{1,2,0:T(8,128)} %get-tuple-element.5) | copy-start | bytes 1572868
  68.6 1.0 copy-start.1
  68.6 1.0 copy-start.7
  72.3 81.7 %reduce-scatter.7.cloned.1.call-start = ((), (), s32[]{:S(2)}) async-start(), calls=%async_computation.4 | async-start | bytes 368640
Sparse Core Ops, SparseCore 0:
  10.2 48.6 all-gather.1
  72.4 59.8 reduce-scatter.4
  134.8 19.2 reduce-scatter.6
where the time goes:
time: 163 us; the launch traced here: 162 us
  waiting for transfers between devices  122 us (75%)
  matrix products  16.5 us (10%)
  between operations  13.9 us (9%)
  local copies, waits for them, and re-layouts  4.77 us (3%)
  other arithmetic  3.24 us (2%)
    reduce_scatter x1, waiting for transfers between devices, on_device(): lax.psum_scatter(jnp.einsum('rc,rd->cd', flat_normed, flat_cot, preferred...  58 us
    all_gather x1, waiting for transfers between devices, on_device(): piece = lax.all_gather(time_weight, 'dp', axis=1, tiled=True)  44.8 us
    unnamed x4, waiting for transfers between devices  19.6 us
    unnamed x18, local copies, waits for them, and re-layouts  4.77 us
    dot_general x3, matrix products, block_tail(): jnp.einsum('fqc,fkc->fqk', queries, keys, preferred_element_type=jnp.floa...  4.1 us
  transfers between devices with their start and end apart: 4, of which 3 were waited for; matrix products, arithmetic and copies ran while one was open for 5% of the time, Pallas kernels for 0%

commit v1 on v0

--- a/solution.py
+++ b/solution.py
@@ -1,8 +1,11 @@
+import functools
 import math
 
 import jax
 import jax.numpy as jnp
 from jax import lax
+from jax.experimental import pallas as pl
+from jax.experimental.pallas import tpu as pltpu
 from jax.sharding import PartitionSpec as P
 
 
@@ -50,7 +53,7 @@
     return (input_grad, normed_bf, qkv_cot)
 
 
-def on_device(clip_input, norm_gain, qkv_weight, out_weight, time_weight, upsample_cotangent):
+def on_device_by_collectives(clip_input, norm_gain, qkv_weight, out_weight, time_weight, upsample_cotangent):
     rows = clip_input[0]
     cotangent = upsample_cotangent[0]
     frames = cotangent.shape[0]
@@ -85,6 +88,447 @@
     return (input_grad[None], qkv_grad)
 
 
+LANES = 128
+MESH = pl.DeviceIdType.MESH
+F32 = jnp.float32
+BF16 = jnp.bfloat16
+
+
+def matmul(a, b, contract):
+    return lax.dot_general(a, b, (contract, ((), ())), preferred_element_type=F32)
+
+
+PLAIN = ((1,), (0,))
+RIGHT_T = ((1,), (1,))
+LEFT_T = ((0,), (0,))
+
+
+def fused_kernel(
+    nz,
+    clip_hbm,
+    gain_ref,
+    qkv_w_hbm,
+    out_w_hbm,
+    taps_hbm,
+    cot_hbm,
+    grad_in_hbm,
+    grad_w_ref,
+    clip,
+    qkv_w,
+    out_w,
+    taps,
+    cot,
+    normed,
+    qkv,
+    probs,
+    upstream,
+    qkv_cot,
+    grad_in,
+    grad,
+    core_in,
+    y_out,
+    y_in,
+    kept,
+    x_out,
+    x_in,
+    z_out,
+    z_in,
+    local_sem,
+    cot_send,
+    cot_recv,
+    z_send,
+    line_recv,
+    x_send,
+    across_recv,
+    pair_send,
+    pair_recv,
+    rs_send,
+    rs_recv,
+):
+    dp, tm = lax.axis_index("dp"), lax.axis_index("tm")
+    z, x = dp // 2, dp % 2
+    y, core = tm // 2, tm % 2
+    frames, hw, width = clip_hbm.shape
+    wide = cot_hbm.shape[-1]
+    half = wide // 2
+    rows = frames * hw
+    cols = width * 3 // 4
+    window = -(-cols // LANES) * LANES
+    stride = cols // LANES * LANES
+    scale = 1.0 / math.sqrt(width)
+    span = nz - 1
+
+    across = (z * 2 + 1 - x, tm)
+    pair = (dp, y * 2 + 1 - core)
+    other_y = (dp, (1 - y) * 2 + core)
+
+    def along_z(d):
+        return ((z + d) * 2 + x, tm)
+
+    def there(d):
+        return jnp.logical_and(z + d >= 0, z + d < nz)
+
+    locals_ = [
+        pltpu.make_async_copy(clip_hbm, clip, local_sem.at[0]),
+        pltpu.make_async_copy(qkv_w_hbm, qkv_w, local_sem.at[1]),
+        pltpu.make_async_copy(taps_hbm, taps.at[dp], local_sem.at[2]),
+        pltpu.make_async_copy(cot_hbm, cot.at[pl.ds(0, frames)], local_sem.at[3]),
+        pltpu.make_async_copy(out_w_hbm, out_w, local_sem.at[4]),
+    ]
+    for copy in locals_:
+        copy.start()
+
+    barrier = pltpu.get_barrier_semaphore()
+    for target in (across, pair, other_y, (dp, 3 - tm)):
+        pl.semaphore_signal(barrier, inc=1, device_id=target, device_id_type=MESH)
+    for d in range(-span, span + 1):
+        if d:
+            pl.when(there(d))(
+                lambda d=d: pl.semaphore_signal(
+                    barrier, inc=1, device_id=along_z(d), device_id_type=MESH
+                )
+            )
+    pl.semaphore_wait(barrier, 4 + span)
+
+    def remote(source, target, send, recv, device):
+        return pltpu.make_async_remote_copy(
+            src_ref=source,
+            dst_ref=target,
+            send_sem=send,
+            recv_sem=recv,
+            device_id=device,
+            device_id_type=MESH,
+        )
+
+    my_half = pl.ds(pl.multiple_of(core * half, LANES), half)
+
+    def slot(line, d):
+        return taps.at[(z + d) * 2 + line, :, :, my_half]
+
+    def held(d):
+        return taps_hbm.at[:, :, my_half] if d == 0 else slot(x, d)
+
+    def z_copy(d, step):
+        return remote(
+            held(d),
+            slot(x, d),
+            z_send.at[(0 if step > 0 else 1), d + span],
+            line_recv.at[d - step + span],
+            along_z(step),
+        )
+
+    def across_copy(d):
+        return remote(held(d), slot(x, d), x_send.at[d + span], across_recv.at[d + span], across)
+
+    def pair_copy(line, d):
+        own = 0 if line == "own" else 1
+        where = slot(x if own == 0 else 1 - x, d)
+        return remote(
+            where, where, pair_send.at[own, d + span], pair_recv.at[own, d + span], pair
+        )
+
+    def line_wait(d):
+        remote(
+            slot(x, d), slot(x, d), z_send.at[0, d + span], line_recv.at[d + span], pair
+        ).wait_recv()
+
+    def across_wait(d):
+        remote(
+            slot(1 - x, d), slot(1 - x, d), x_send.at[d + span], across_recv.at[d + span], across
+        ).wait_recv()
+
+    pair_incoming = []
+
+    cot_copy = remote(
+        cot_hbm, cot.at[pl.ds(frames, frames)], cot_send.at[0], cot_recv.at[0], (dp, tm - 1)
+    )
+
+    def start_when(condition, copy):
+        pl.when(condition)(lambda: copy().start())
+
+    start_when(tm > 0, lambda: cot_copy)
+    start_when(there(1), lambda: z_copy(0, 1))
+    start_when(there(-1), lambda: z_copy(0, -1))
+    across_copy(0).start()
+
+    def pass_on(d):
+        def go():
+            line_wait(d)
+            step = 1 if d < 0 else -1
+            start_when(there(step), lambda: z_copy(d, step))
+            across_copy(d).start()
+            pair_copy("own", d).start()
+
+        pl.when(there(d))(go)
+
+    def pass_across(d):
+        def go():
+            across_wait(d)
+            pair_copy("other", d).start()
+
+        pl.when(there(d))(go)
+
+    def project():
+        locals_[0].wait()
+        locals_[1].wait()
+        features = clip[...].reshape(rows, width).astype(F32)
+        squares = jnp.mean(features * features, axis=-1, keepdims=True)
+        normed[...] = (features * lax.rsqrt(squares + 1e-06) * gain_ref[...]).astype(BF16)
+        qkv[...] = matmul(normed[...], qkv_w[...], PLAIN).astype(BF16)
+
+    def attend(f):
+        at = pl.ds(f * hw, hw)
+        scores = matmul(qkv[at, 0:width], qkv[at, width : 2 * width], RIGHT_T) * scale
+        weights = jnp.exp(scores - jnp.max(scores, axis=-1, keepdims=True))
+        probs[f] = weights / jnp.sum(weights, axis=-1, keepdims=True)
+
+    @pl.when(tm == 3)
+    def _():
+        cot[frames : 2 * frames] = jnp.zeros((frames, hw, wide), BF16)
+
+    work = [project] + [functools.partial(attend, f) for f in range(frames)]
+    for k in range(1, nz):
+        if work:
+            work.pop(0)()
+        pass_on(-k)
+        pass_on(k)
+        for d in sorted({-(k - 1), k - 1}):
+            pass_across(d)
+    for step in work:
+        step()
+    for d in (-span, span):
+        pass_across(d)
+
+    locals_[2].wait()
+    locals_[3].wait()
+    locals_[4].wait()
+    pl.when(tm < 3)(lambda: cot_copy.wait_recv())
+    pair_half = pl.ds(pl.multiple_of((1 - core) * half, LANES), half)
+
+    def pair_wait(line, own, d):
+        where = taps.at[(z + d) * 2 + line, :, :, pair_half]
+        remote(
+            where, where, pair_send.at[own, d + span], pair_recv.at[own, d + span], pair
+        ).wait_recv()
+
+    for d in range(-span, span + 1):
+        if d:
+            pl.when(there(d))(lambda d=d: pair_wait(x, 0, d))
+        pl.when(there(d))(lambda d=d: pair_wait(1 - x, 1, d))
+
+    total = None
+    for tap in range(3):
+        part = matmul(
+            cot[2 - tap : 2 - tap + frames].reshape(rows, wide),
+            taps[:, tap].reshape(width, wide),
+            RIGHT_T,
+        )
+        total = part if total is None else total + part
+    upstream[...] = total.astype(BF16)
+    mixed_cot = matmul(upstream[...], out_w[...], RIGHT_T).astype(BF16)
+    for f in range(frames):
+        at = pl.ds(f * hw, hw)
+        p = probs[f]
+        d_mixed = mixed_cot[f * hw : (f + 1) * hw]
+        qkv_cot[at, 2 * width : 3 * width] = matmul(p.astype(BF16), d_mixed, LEFT_T).astype(BF16)
+        d_weights = matmul(d_mixed, qkv[at, 2 * width : 3 * width], RIGHT_T)
+        d_weights = d_weights.astype(BF16).astype(F32)
+        inner = jnp.sum(p * d_weights, axis=-1, keepdims=True)
+        d_scores = (p * (d_weights - inner) * scale).astype(BF16)
+        qkv_cot[at, 0:width] = matmul(d_scores, qkv[at, width : 2 * width], PLAIN).astype(BF16)
+        qkv_cot[at, width : 2 * width] = matmul(d_scores, qkv[at, 0:width], LEFT_T).astype(BF16)
+
+    grad[...] = (
+        matmul(normed[...], qkv_cot[...], LEFT_T).astype(BF16).reshape(nz, 2, -1, 3 * width)
+    )
+
+    def columns(t):
+        return pl.ds(pl.multiple_of(t * stride, LANES), window)
+
+    def core_copy(i, side):
+        return remote(
+            grad.at[:, :, :, columns(side * 2 + 1 - core)],
+            core_in.at[i],
+            rs_send.at[i],
+            rs_recv.at[i],
+            pair,
+        )
+
+    core_copies = [core_copy(0, 1 - y), core_copy(1, y)]
+    for copy in core_copies:
+        copy.start()
+    y_copies = [
+        remote(y_out.at[i], y_in.at[i], rs_send.at[2 + i], rs_recv.at[2 + i], other_y)
+        for i in range(2)
+    ]
+    core_copies[0].wait_recv()
+    for i, line in enumerate((1 - x, x)):
+        y_out[i] = (
+            grad[:, line, :, columns((1 - y) * 2 + core)].astype(F32)
+            + core_in[0, :, line].astype(F32)
+        ).astype(BF16)
+        y_copies[i].start()
+    core_copies[1].wait_recv()
+    for i, line in enumerate((1 - x, x)):
+        kept[i] = grad[:, line, :, columns(tm)].astype(F32) + core_in[1, :, line].astype(F32)
+
+    features = clip[...].reshape(rows, width).astype(F32)
+    squares = jnp.mean(features * features, axis=-1, keepdims=True)
+    root = lax.rsqrt(squares + 1e-06)
+    scaled = matmul(qkv_cot[...], qkv_w[...], RIGHT_T) * gain_ref[...]
+    lean = jnp.mean(features * scaled, axis=-1, keepdims=True)
+    direct = root * scaled - features * (root * root * root * lean)
+    grad_in[...] = (
+        (upstream[...].astype(F32) + direct).astype(BF16).reshape(frames, hw, width)
+    )
+    result_copy = pltpu.make_async_copy(grad_in, grad_in_hbm, local_sem.at[5])
+    result_copy.start()
+
+    x_copy = remote(x_out, x_in, rs_send.at[4], rs_recv.at[4], across)
+    y_copies[0].wait_recv()
+    x_out[...] = (kept[0] + y_in[0].astype(F32)).astype(BF16)
+    x_copy.start()
+    y_copies[1].wait_recv()
+    kept[1] = kept[1] + y_in[1].astype(F32)
+    x_copy.wait_recv()
+    kept[1] = kept[1] + x_in[...].astype(F32)
+    z_out[...] = kept[1].astype(BF16)
+
+    def z_share(d):
+        return remote(
+            z_out.at[z + d],
+            z_in.at[span - d],
+            rs_send.at[5 + span + d],
+            rs_recv.at[5 + span - d],
+            along_z(d),
+        )
+
+    def z_wait(d):
+        remote(
+            z_in.at[span + d],
+            z_in.at[span + d],
+            rs_send.at[5 + span + d],
+            rs_recv.at[5 + span + d],
+            along_z(d),
+        ).wait_recv()
+
+    distances = [d for k in range(span, 0, -1) for d in (-k, k)]
+    for d in distances:
+        start_when(there(d), lambda d=d: z_share(d))
+    kept[0, 0] = kept[1, z]
+    for d in reversed(distances):
+
+        @pl.when(there(d))
+        def _(d=d):
+            z_wait(d)
+            kept[0, 0] = kept[0, 0] + z_in[span + d].astype(F32)
+
+    for t in range(4):
+
+        @pl.when(tm == t)
+        def _(t=t):
+            first = t * (cols - stride)
+            grad_w_ref[...] = kept[0, 0][:, first : first + cols]
+
+    pl.when(tm > 0)(lambda: cot_copy.wait_send())
+    across_copy(0).wait_send()
+    for step in (1, -1):
+        pl.when(there(step))(lambda step=step: z_copy(0, step).wait_send())
+    for d in range(-span, span + 1):
+
+        @pl.when(there(d))
+        def _(d=d):
+            if d:
+                step = 1 if d < 0 else -1
+                if abs(d) < span:
+                    pl.when(there(step))(lambda: z_copy(d, step).wait_send())
+                across_copy(d).wait_send()
+                pair_copy("own", d).wait_send()
+                z_share(d).wait_send()
+            pair_copy("other", d).wait_send()
+
+    for copy in core_copies + y_copies + [x_copy]:
+        copy.wait_send()
+    result_copy.wait()
+
+
+def on_device(ndp, ntm, clip_input, norm_gain, qkv_weight, out_weight, time_weight, upsample_cotangent):
+    _, frames, hw, width = clip_input.shape
+    wide = upsample_cotangent.shape[-1]
+    share = width // ndp
+    fits = ndp % 2 == 0 and ntm == 4 and frames == 2 and share % 16 == 0
+    if not fits or width % LANES or wide % (2 * LANES):
+        return on_device_by_collectives(
+            clip_input, norm_gain, qkv_weight, out_weight, time_weight, upsample_cotangent
+        )
+    nz = ndp // 2
+    cols = 3 * width // ntm
+    window = -(-cols // LANES) * LANES
+    rows = frames * hw
+    steps = 2 * nz - 1
+    anywhere = pl.BlockSpec(memory_space=pl.ANY)
+    vmem = pl.BlockSpec(memory_space=pltpu.VMEM)
+    dma = pltpu.SemaphoreType.DMA
+    grad_in, grad_w = pl.pallas_call(
+        functools.partial(fused_kernel, nz),
+        out_shape=(
+            jax.ShapeDtypeStruct((frames, hw, width), BF16),
+            jax.ShapeDtypeStruct((share, cols), F32),
+        ),
+        in_specs=[anywhere, vmem, anywhere, anywhere, anywhere, anywhere],
+        out_specs=(anywhere, vmem),
+        scratch_shapes=[
+            pltpu.VMEM((frames, hw, width), BF16),
+            pltpu.VMEM((width, 3 * width), BF16),
+            pltpu.VMEM((width, width), BF16),
+            pltpu.VMEM((ndp, 3, share, wide), BF16),
+            pltpu.VMEM((2 * frames, hw, wide), BF16),
+            pltpu.VMEM((rows, width), BF16),
+            pltpu.VMEM((rows, 3 * width), BF16),
+            pltpu.VMEM((frames, hw, hw), F32),
+            pltpu.VMEM((rows, width), BF16),
+            pltpu.VMEM((rows, 3 * width), BF16),
+            pltpu.VMEM((frames, hw, width), BF16),
+            pltpu.VMEM((nz, 2, share, 3 * width), BF16),
+            pltpu.VMEM((2, nz, 2, share, window), BF16),
+            pltpu.VMEM((2, nz, share, window), BF16),
+            pltpu.VMEM((2, nz, share, window), BF16),
+            pltpu.VMEM((2, nz, share, window), F32),
+            pltpu.VMEM((nz, share, window), BF16),
+            pltpu.VMEM((nz, share, window), BF16),
+            pltpu.VMEM((nz, share, window), BF16),
+            pltpu.VMEM((steps, share, window), BF16),
+            dma((6,)),
+            dma((1,)),
+            dma((1,)),
+            dma((2, steps)),
+            dma((steps,)),
+            dma((steps,)),
+            dma((steps,)),
+            dma((2, steps)),
+            dma((2, steps)),
+            dma((5 + steps,)),
+            dma((5 + steps,)),
+        ],
+        compiler_params=pltpu.CompilerParams(
+            collective_id=0, has_side_effects=True, vmem_limit_bytes=50 * 1024 * 1024
+        ),
+        cost_estimate=pl.CostEstimate(
+            flops=2 * rows * width * (3 * wide + 10 * width + 6 * hw),
+            bytes_accessed=4 * rows * wide + 16 * width * width,
+            transcendentals=rows * hw,
+        ),
+    )(
+        clip_input[0],
+        norm_gain.reshape(1, width),
+        qkv_weight,
+        out_weight,
+        time_weight,
+        upsample_cotangent[0],
+    )
+    return (grad_in[None], grad_w)
+
+
 def solution(mesh):
     in_specs = (
         P("dp", "tm", None, None),
@@ -96,5 +540,9 @@
     )
     out_specs = (P("dp", "tm", None, None), P("dp", "tm"))
     return jax.shard_map(
-        on_device, mesh=mesh, in_specs=in_specs, out_specs=out_specs, check_vma=False
-    )
+        functools.partial(on_device, mesh.shape["dp"], mesh.shape["tm"]),
+        mesh=mesh,
+        in_specs=in_specs,
+        out_specs=out_specs,
+        check_vma=False,
+    )

time: 163 us -> 50.2 us (0.31)
  waiting for transfers between devices: 122 us -> 0 us
  Pallas kernels: 0 us -> 41.9 us
  matrix products: 16.5 us -> 0 us
  between operations: 13.9 us -> 0.65 us
  other arithmetic: 3.24 us -> 0 us
  local copies, waits for them, and re-layouts: 4.77 us -> 7.25 us
    reduce_scatter x1 -> x0, waiting for transfers between devices: 58 us -> none  [on_device(): lax.psum_scatter(jnp.einsum('rc,rd->cd', flat_normed, flat_cot, preferred...]
    all_gather x1 -> x0, waiting for transfers between devices: 44.8 us -> none  [on_device(): piece = lax.all_gather(time_weight, 'dp', axis=1, tiled=True)]
    pallas_call x0 -> x1, Pallas kernels: none -> 41.9 us  [on_device(): pl.pallas_call(functools.partial(fused_kernel, nz), out_shape=(jax.ShapeD...]
    unnamed x4 -> x0, waiting for transfers between devices: 19.6 us -> none
    dot_general x12 -> x0, matrix products: 16.5 us -> none  [the longest x3 4.1 us: block_tail(): jnp.einsum('fqc,fkc->fqk', queries, keys, preferred_element_type=jnp.floa...]
    unnamed x18 -> x14, local copies, waits for them, and re-layouts: 4.77 us -> 7.25 us
  transfers between devices with their start and end apart: 4 -> 0, of which waited for: 3 -> 0; matrix products, arithmetic and copies ran while one was open for 5% -> 0% of each run, Pallas kernels for 0% -> 0%
where the time goes in v1:
time: 50.2 us; the launch traced here: 49.8 us
  Pallas kernels  41.9 us (83%)
  local copies, waits for them, and re-layouts  7.25 us (14%)
  between operations  0.65 us (1%)
    pallas_call x1, Pallas kernels, on_device(): pl.pallas_call(functools.partial(fused_kernel, nz), out_shape=(jax.ShapeD...  41.9 us
    unnamed x14, local copies, waits for them, and re-layouts  7.25 us

profile of v1, /device:TPU:0, one launch (start us, length us, event | category | flops | bytes accessed | tf_op | source)
XLA Modules:
  0.0 49.8 jit_solution(7746240055797293449)
XLA Ops:
  0.6 0.0 copy-start.5
  0.6 0.7 %copy-done.5 = f32[384]{0:T(512)S(1)} copy-done((f32[384]{0:T(512)S(1)}, f32[384]{0:T(512)}, u32[]{:S(2)}) %copy-start.5) | copy-done | bytes 1560
  1.3 0.0 copy-start
  1.3 1.2 %copy-done = bf16[384,1152]{1,0:T(8,128)(2,1)S(1)} copy-done((bf16[384,1152]{1,0:T(8,128)(2,1)S(1)}, bf16[384,1152]{1,0:T(8,128)(2,1)}, u32[]{:S(2)}) %copy-start) | copy-done | bytes 884760
  2.5 0.0 copy-start.1
  2.5 1.1 %copy-done.1 = bf16[1,2,256,768]{3,2,1,0:T(8,128)(2,1)S(1)} copy-done((bf16[1,2,256,768]{3,2,1,0:T(8,128)(2,1)S(1)}, bf16[1,2,256,768]{3,2,1,0:T(8,128)(2,1)}, u32[]{:S(2)}) %copy-start.1) | copy-done | bytes 786456
  3.6 0.0 copy-start.2
  3.6 1.0 %copy-done.2 = bf16[1,2,256,384]{3,2,1,0:T(8,128)(2,1)S(1)} copy-done((bf16[1,2,256,384]{3,2,1,0:T(8,128)(2,1)S(1)}, bf16[1,2,256,384]{3,2,1,0:T(8,128)(2,1)}, u32[]{:S(2)}) %copy-start.2) | copy-done | bytes 393240
  4.6 0.0 copy-start.3
  4.6 1.0 %copy-done.3 = bf16[384,384]{1,0:T(8,128)(2,1)S(1)} copy-done((bf16[384,384]{1,0:T(8,128)(2,1)S(1)}, bf16[384,384]{1,0:T(8,128)(2,1)}, u32[]{:S(2)}) %copy-start.3) | copy-done | bytes 294936
  5.6 0.0 copy-start.4
  5.6 0.9 %copy-done.4 = bf16[3,48,768]{2,1,0:T(8,128)(2,1)S(1)} copy-done((bf16[3,48,768]{2,1,0:T(8,128)(2,1)S(1)}, bf16[3,48,768]{2,1,0:T(8,128)(2,1)}, u32[]{:S(2)}) %copy-start.4) | copy-done | bytes 221208
  6.5 41.9 %shard_map.77 = (bf16[2,256,384]{2,1,0:T(8,128)(2,1)S(1)}, f32[48,288]{1,0:T(8,128)S(1)}) custom-call(bf16[2,256,384]{2,1,0:T(8,128)(2,1)S(1)} %bitcast.5, f32[1,384]{1,0:T(1,128)S(1)} %reshape.7.gain_ref, bf16[384,1152]{1,0:T(8,128)(2,1)S(1)} %copy-done, bf16[384,384]{1,0:T(8,128)(2,1)S(1)} %copy-done.3, bf16[3,48,768]{2,1,0:T(8,128)(2,1)S(1)} %copy-done.4, ...), custom_call_target="tpu_custom_call" | custom-call | flops 3019898880 | bytes 3932160 | tf_op jit(solution)/shard_map/pallas_call | solution.py:472
  48.5 0.7 %copy.10 = bf16[1,2,256,384]{3,2,1,0:T(8,128)(2,1)} copy(bf16[1,2,256,384]{3,2,1,0:T(8,128)(2,1)S(1)} %bitcast.3) | data formatting | bytes 786432
  49.2 0.6 %copy.11 = f32[48,288]{1,0:T(8,128)} copy(f32[48,288]{1,0:T(8,128)S(1)} %get-tuple-element.9) | data formatting | bytes 110592
  (1 shorter events, 0.0 us)
Async XLA Ops:
  0.6 0.7 %copy-start.5 = (f32[384]{0:T(512)S(1)}, f32[384]{0:T(512)}, u32[]{:S(2)}) copy-start(f32[384]{0:T(512)} %param.7) | copy-start | bytes 4612
  1.3 1.2 %copy-start = (bf16[384,1152]{1,0:T(8,128)(2,1)S(1)}, bf16[384,1152]{1,0:T(8,128)(2,1)}, u32[]{:S(2)}) copy-start(bf16[384,1152]{1,0:T(8,128)(2,1)} %qkv_w_hbm.1) | copy-start | bytes 2654212
  2.5 1.1 %copy-start.1 = (bf16[1,2,256,768]{3,2,1,0:T(8,128)(2,1)S(1)}, bf16[1,2,256,768]{3,2,1,0:T(8,128)(2,1)}, u32[]{:S(2)}) copy-start(bf16[1,2,256,768]{3,2,1,0:T(8,128)(2,1)} %param.11) | copy-start | bytes 2359300
  3.6 1.0 %copy-start.2 = (bf16[1,2,256,384]{3,2,1,0:T(8,128)(2,1)S(1)}, bf16[1,2,256,384]{3,2,1,0:T(8,128)(2,1)}, u32[]{:S(2)}) copy-start(bf16[1,2,256,384]{3,2,1,0:T(8,128)(2,1)} %param.6) | copy-start | bytes 1179652
  4.6 1.0 %copy-start.3 = (bf16[384,384]{1,0:T(8,128)(2,1)S(1)}, bf16[384,384]{1,0:T(8,128)(2,1)}, u32[]{:S(2)}) copy-start(bf16[384,384]{1,0:T(8,128)(2,1)} %out_w_hbm.1) | copy-start | bytes 884740
  5.6 0.9 %copy-start.4 = (bf16[3,48,768]{2,1,0:T(8,128)(2,1)S(1)}, bf16[3,48,768]{2,1,0:T(8,128)(2,1)}, u32[]{:S(2)}) copy-start(bf16[3,48,768]{2,1,0:T(8,128)(2,1)} %taps_hbm.1) | copy-start | bytes 663556
